TPU v7x, 512 devices: a whole 4x8x8 slice. The times are simulated.
512 devices in a mesh: ctx: 64 (over y_lo, z, x), tp: 8 (over y_hi, core).
Axes of the slice: x: 4, y: 8 (y_hi: 4, y_lo: 2; y = y_hi * 2 + y_lo), z: 8, core: 2. Of those that a mesh axis runs over, the one named last changes fastest.
Arguments:
- queries: bfloat16 [16384, 8192], P('ctx', 'tp'), may hold values from -128 to 128
- cotangent: bfloat16 [16384, 8192], P('ctx', 'tp'), may hold values from -96 to 96
- image_keys: bfloat16 [64, 64, 1024], P('ctx', None, 'tp'), may hold values from -8 to 8
- image_values: bfloat16 [64, 64, 1024], P('ctx', None, 'tp'), may hold values from -6 to 6
- attn_gate: float32 [1], replicated, may hold values from 0.4 to 1.5
- block_mask: int32 [128, 64], P('ctx'), may hold values from 0 to 1, as said below
- image_owner: int32 [64], replicated, may hold values from 0 to 63, each once
Outputs:
- query_grad: bfloat16 [16384, 8192], P('ctx', 'tp')
- key_grad: bfloat16 [64, 64, 1024], P('ctx', None, 'tp')
- value_grad: bfloat16 [64, 64, 1024], P('ctx', None, 'tp')
- gate_grad: float32 [1], replicated
Inputs may be any that keep to these rules, and one draw needn't show every extreme that they name: `block_mask`: every text block reads at least one image; the 2 blocks of one index of ctx together read exactly 32 distinct images.
All inputs are finite; a program needn't handle non-finite values.
Results may differ from a plain program's by a relative error of at most 0.02.
Values may be sent and summed in bfloat16 or wider, within the bound.
A program may use at most 64 MiB of HBM per device.

v0:
```python
import math
import jax
import jax.numpy as jnp
from jax import lax
from jax.sharding import PartitionSpec as P

HD = 128
BLK = 128


def per_device(queries, cotangent, image_keys, image_values, attn_gate, block_mask, image_owner):
    tok_dev = queries.shape[0]
    local_kv = image_keys.shape[2] // HD
    local_heads = queries.shape[1] // HD
    groups = local_heads // local_kv
    img_tok = image_keys.shape[1]
    inv_root = 1.0 / math.sqrt(HD)
    read_most = lax.axis_size("ctx") // 2
    gathered_keys, gathered_values = (
        lax.all_gather(image_keys, "ctx", axis=0, tiled=True),
        lax.all_gather(image_values, "ctx", axis=0, tiled=True),
    )
    n_images = gathered_keys.shape[0]
    read_any = jnp.max(block_mask, axis=0)
    ranking = read_any * (2 * n_images) + (n_images - 1 - jnp.arange(n_images, dtype=jnp.int32))
    top_vals, image_ids = lax.top_k(ranking, read_most)
    is_read = read_any[image_ids] > 0
    slot_ids = image_owner[image_ids]
    block_keep = (block_mask[:, image_ids] > 0) & is_read[None, :]
    keep_mask = jnp.repeat(jnp.repeat(block_keep, BLK, axis=0), img_tok, axis=1)
    key_rows = jnp.take(gathered_keys, slot_ids, axis=0).reshape(read_most * img_tok, local_kv, HD)
    value_rows = jnp.take(gathered_values, slot_ids, axis=0).reshape(
        read_most * img_tok, local_kv, HD
    )
    query_heads = queries.reshape(tok_dev, local_kv, groups, HD).transpose(2, 0, 1, 3)
    cot_heads = cotangent.reshape(tok_dev, local_kv, groups, HD).transpose(2, 0, 1, 3)
    gate_value = jnp.tanh(attn_gate[0])

    def head_step(state_in, head_inputs):
        key_acc, value_acc, gate_acc = state_in
        query_one, cot_one = head_inputs
        scores = (
            jnp.einsum("tkd,skd->kts", query_one, key_rows, preferred_element_type=jnp.float32)
            * inv_root
        )
        scores = jnp.where(keep_mask, scores, -1e30)
        row_max = jnp.max(scores, axis=-1, keepdims=True)
        exp_terms = jnp.where(keep_mask, jnp.exp(scores - row_max), 0.0)
        prob_full = exp_terms / jnp.sum(exp_terms, axis=-1, keepdims=True)
        prob_half = prob_full.astype(jnp.bfloat16)
        attended = jnp.einsum(
            "kts,skd->tkd", prob_half, value_rows, preferred_element_type=jnp.float32
        )
        cot_f = cot_one.astype(jnp.float32)
        gate_part = jnp.sum(cot_f * attended)
        attn_grad = (gate_value * cot_f).astype(jnp.bfloat16)
        prob_grad = jnp.einsum(
            "tkd,skd->kts", attn_grad, value_rows, preferred_element_type=jnp.float32
        )
        row_delta = jnp.sum(attn_grad.astype(jnp.float32) * attended, axis=-1).T
        score_grad = (prob_full * (prob_grad - row_delta[:, :, None]) * inv_root).astype(
            jnp.bfloat16
        )
        query_grad = jnp.einsum(
            "kts,skd->tkd", score_grad, key_rows, preferred_element_type=jnp.float32
        ).astype(jnp.bfloat16)
        key_acc = key_acc + jnp.einsum(
            "kts,tkd->skd", score_grad, query_one, preferred_element_type=jnp.float32
        )
        value_acc = value_acc + jnp.einsum(
            "kts,tkd->skd", prob_half, attn_grad, preferred_element_type=jnp.float32
        )
        return ((key_acc, value_acc, gate_acc + gate_part), query_grad)

    zero_grads = jnp.zeros((read_most * img_tok, local_kv, HD), jnp.float32)
    init_state = (zero_grads, zero_grads, jnp.zeros((), jnp.float32))
    (key_acc, value_acc, gate_acc), head_grads = lax.scan(
        head_step, init_state, (query_heads, cot_heads)
    )
    query_grad = head_grads.transpose(1, 2, 0, 3).reshape(tok_dev, local_heads * HD)
    stacked = jnp.concatenate(
        [
            key_acc.reshape(read_most, img_tok, local_kv * HD),
            value_acc.reshape(read_most, img_tok, local_kv * HD),
        ],
        axis=-1,
    )
    stacked = jnp.where(is_read[:, None, None], stacked, 0.0)
    buffer = (
        jnp.zeros((n_images, img_tok, 2 * local_kv * HD), jnp.float32).at[slot_ids].add(stacked)
    )
    received = lax.all_to_all(buffer, "ctx", split_axis=0, concat_axis=0, tiled=True)
    summed = jnp.sum(received, axis=0, keepdims=True)
    key_grad = summed[:, :, : local_kv * HD].astype(jnp.bfloat16)
    value_grad = summed[:, :, local_kv * HD :].astype(jnp.bfloat16)
    gate_total = lax.psum(gate_acc, ("ctx", "tp"))
    term_count = tok_dev * lax.axis_size("ctx") * local_heads * lax.axis_size("tp") * HD
    gate_grad = ((1.0 - gate_value * gate_value) * gate_total / math.sqrt(term_count)).reshape(1)
    return (query_grad, key_grad, value_grad, gate_grad)


def solution(mesh):
    in_specs = (
        P("ctx", "tp"),
        P("ctx", "tp"),
        P("ctx", None, "tp"),
        P("ctx", None, "tp"),
        P(),
        P("ctx", None),
        P(),
    )
    out_specs = (P("ctx", "tp"), P("ctx", None, "tp"), P("ctx", None, "tp"), P())
    return jax.shard_map(
        per_device, mesh=mesh, in_specs=in_specs, out_specs=out_specs, check_vma=False
    )
```

profile of v0, /device:TPU:1, one launch (start us, length us, event | category | flops | bytes accessed | tf_op | source)
XLA Modules:
  0.0 885.6 jit_solution(12151461978923027463)
XLA Ops:
  10.9 2.0 top_k.11
  17.4 253.3 %all-gather.5.cloned.1.call-done = bf16[64,64,128]{2,1,0:T(8,128)(2,1)} async-done(((bf16[1,64,128]{2,1,0:T(8,128)(2,1)}), bf16[64,64,128]{2,1,0:T(8,128)(2,1)}) %all-gather.5.cloned.1.call-update) | async-done | bytes 1048592 | tf_op jit(solution)/shard_map/all_gather | solution.py:21
  270.7 1.9 gather_fusion.4
  272.6 297.7 %all-gather.3.cloned.1.call-done = bf16[64,64,128]{2,1,0:T(8,128)(2,1)} async-done(((bf16[1,64,128]{2,1,0:T(8,128)(2,1)}), bf16[64,64,128]{2,1,0:T(8,128)(2,1)}) %all-gather.3.cloned.1.call-update) | async-done | bytes 1048592 | tf_op jit(solution)/shard_map/all_gather | solution.py:20
  570.4 1.9 gather_fusion.3
  572.4 92.9 %while.17 = (s32[]{:T(128)}, f32[2048,1,128]{0,2,1:T(8,128)}, f32[2048,1,128]{0,2,1:T(8,128)}, f32[]{:T(128)}, bf16[8,256,1,128]{3,1,2,0:T(8,128)(2,1)}, /*index...) while((s32[]{:T(128)}, f32[2048,1,128]{0,2,1:T(8,128)}, ...), condition=%wide.region_7.9_spmd.clone, body=%wide.region_2.8_spmd.clone.sunk | while | flops 814710016 | bytes 48644448 | solution.py:77
  575.2 1.9 fusion.68
  577.8 1.4 fusion.69
  586.8 1.9 fusion.68
  598.4 1.9 fusion.68
  610.1 1.9 fusion.68
  612.7 1.4 fusion.69
  621.7 1.9 fusion.68
  633.3 1.9 fusion.68
  635.9 1.4 fusion.69
  644.9 1.9 fusion.68
  656.5 1.9 fusion.68
  665.3 1.6 copy.40
  668.3 1.4 maximum_select_fusion
  669.8 2.5 broadcast_in_dim.68
  672.2 6.4 scatter_fusion
  678.6 7.4 all-to-all-start
  686.0 186.7 %psum.7 = f32[]{:T(128)} all-reduce(f32[]{:T(128)} %get-tuple-element.72), channel_id=1, replica_groups=mesh['ctx'=64,'tp'=8] {'ctx','tp'}, use_global_device_ids=true, to_apply=%region_10.12 | all-reduce | flops 1 | bytes 8 | tf_op jit(solution)/shard_map/psum | solution.py:96
  874.6 2.4 reduce_sum.36
  (205 shorter events, 77.7 us)
Async XLA Ops:
  7.2 6.5 copy-start
  7.2 9.2 %copy-start.8 = (bf16[256,1024]{1,0:T(8,128)(2,1)S(1)}, bf16[256,1024]{1,0:T(8,128)(2,1)}, u32[]{:S(2)}) copy-start(bf16[256,1024]{1,0:T(8,128)(2,1)} %param.12) | copy-start | bytes 1572868
  7.2 263.5 %all-gather.5.cloned.1.call-start = ((), (), s32[]{:S(2)}) async-start(), calls=%async_computation.2 | async-start | bytes 1064960 | tf_op jit(solution)/shard_map/all_gather | solution.py:21
  7.9 562.4 %all-gather.3.cloned.1.call-start = ((), (), s32[]{:S(2)}) async-start(), calls=%async_computation.1 | async-start | bytes 1064960 | tf_op jit(solution)/shard_map/all_gather | solution.py:20
  579.3 2.5 copy-start.4
  580.7 2.4 copy-start.2
  580.7 3.4 copy-start.7
  590.9 2.5 copy-start.4
  592.3 3.4 copy-start.7
  602.5 2.5 copy-start.4
  603.9 2.4 copy-start.2
  603.9 3.4 copy-start.7
  614.1 2.5 copy-start.4
  615.5 3.4 copy-start.7
  625.7 2.5 copy-start.4
  627.1 3.4 copy-start.7
  637.3 2.5 copy-start.4
  638.7 3.4 copy-start.7
  649.0 2.5 copy-start.4
  650.4 3.4 copy-start.7
  660.6 2.5 copy-start.4
  662.0 3.4 copy-start.7
  678.6 194.1 %copy-start.9 = (bf16[8,256,1,128]{3,1,2,0:T(8,128)(2,1)S(1)}, bf16[8,256,1,128]{3,1,2,0:T(8,128)(2,1)}, u32[]{:S(2)}) copy-start(bf16[8,256,1,128]{3,1,2,0:T(8,128)(2,1)} %get-tuple-element.69) | copy-start | bytes 1572868
  678.6 196.0 %all-to-all-start = ((f32[64,64,256]{2,1,0:T(8,128)}), f32[64,64,256]{2,1,0:T(8,128)}, u32[]{:S(2)}, u32[]{:S(2)}) async-start(f32[64,64,256]{2,1,0:T(8,128)} %scatter_fusion), calls=%async_computation | async-start | bytes 8388608 | tf_op jit(solution)/shard_map/all_to_all | solution.py:92
  (31 other events, 46.7 us)
Sparse Core Ops, SparseCore 0:
  10.1 260.5 all-gather.4
  272.8 297.4 all-gather.2
where the time goes:
time: 887 us; the launch traced here: 886 us
  waiting for transfers between devices  552 us (62%)
  blocking collectives  187 us (21%)
  matrix products  61.8 us (7%)
  local copies, waits for them, and re-layouts  30.3 us (3%)
  other arithmetic  24.2 us (3%)
  between operations  16.7 us (2%)
    all_gather x1, waiting for transfers between devices, per_device(): lax.all_gather(image_keys, 'ctx', axis=0, tiled=True)  298 us
    all_gather x1, waiting for transfers between devices, per_device(): lax.all_gather(image_values, 'ctx', axis=0, tiled=True)  253 us
    psum x1, blocking collectives, per_device(): gate_total = lax.psum(gate_acc, ('ctx', 'tp'))  187 us
  transfers between devices with their start and end apart: 3, of which 2 were waited for; matrix products, arithmetic and copies ran while one was open for 1% of the time, Pallas kernels for 0%

commit v1 on v0

--- a/solution.py
+++ b/solution.py
@@ -93,7 +93,7 @@
     summed = jnp.sum(received, axis=0, keepdims=True)
     key_grad = summed[:, :, : local_kv * HD].astype(jnp.bfloat16)
     value_grad = summed[:, :, local_kv * HD :].astype(jnp.bfloat16)
-    gate_total = lax.psum(gate_acc, ("ctx", "tp"))
+    gate_total = jnp.sum(lax.all_gather(gate_acc, ("ctx", "tp")), axis=0)
     term_count = tok_dev * lax.axis_size("ctx") * local_heads * lax.axis_size("tp") * HD
     gate_grad = ((1.0 - gate_value * gate_value) * gate_total / math.sqrt(term_count)).reshape(1)
     return (query_grad, key_grad, value_grad, gate_grad)

time: 887 us -> 888 us (level)
    psum x1 -> x0, blocking collectives: 187 us -> none  [per_device(): gate_total = lax.psum(gate_acc, ('ctx', 'tp'))]
    unnamed x0 -> x1, blocking collectives: none -> 187 us
where the time goes in v1:
time: 888 us; the launch traced here: 886 us
  waiting for transfers between devices  552 us (62%)
  blocking collectives  187 us (21%)
  matrix products  61.8 us (7%)
  local copies, waits for them, and re-layouts  30.4 us (3%)
  other arithmetic  24.8 us (3%)
  between operations  16.7 us (2%)
    all_gather x1, waiting for transfers between devices, per_device(): lax.all_gather(image_keys, 'ctx', axis=0, tiled=True)  298 us
    all_gather x1, waiting for transfers between devices, per_device(): lax.all_gather(image_values, 'ctx', axis=0, tiled=True)  253 us
    unnamed x1, blocking collectives  187 us
  transfers between devices with their start and end apart: 3, of which 2 were waited for; matrix products, arithmetic and copies ran while one was open for 1% of the time, Pallas kernels for 0%

profile of v1, /device:TPU:1, one launch (start us, length us, event | category | flops | bytes accessed | tf_op | source)
XLA Modules:
  0.0 886.3 jit_solution(6285216931357811261)
XLA Ops:
  10.9 2.0 top_k.11
  17.4 253.3 %all-gather.5.cloned.1.call-done = bf16[64,64,128]{2,1,0:T(8,128)(2,1)} async-done(((bf16[1,64,128]{2,1,0:T(8,128)(2,1)}), bf16[64,64,128]{2,1,0:T(8,128)(2,1)}) %all-gather.5.cloned.1.call-update) | async-done | bytes 1048592 | tf_op jit(solution)/shard_map/all_gather | solution.py:21
  270.7 1.9 gather_fusion.4
  272.6 297.7 %all-gather.3.cloned.1.call-done = bf16[64,64,128]{2,1,0:T(8,128)(2,1)} async-done(((bf16[1,64,128]{2,1,0:T(8,128)(2,1)}), bf16[64,64,128]{2,1,0:T(8,128)(2,1)}) %all-gather.3.cloned.1.call-update) | async-done | bytes 1048592 | tf_op jit(solution)/shard_map/all_gather | solution.py:20
  570.4 1.9 gather_fusion.3
  572.4 92.9 %while.17 = (s32[]{:T(128)}, f32[2048,1,128]{0,2,1:T(8,128)}, f32[2048,1,128]{0,2,1:T(8,128)}, f32[]{:T(128)}, bf16[8,256,1,128]{3,1,2,0:T(8,128)(2,1)}, /*index...) while((s32[]{:T(128)}, f32[2048,1,128]{0,2,1:T(8,128)}, ...), condition=%wide.region_7.9_spmd.clone, body=%wide.region_2.8_spmd.clone.sunk | while | flops 814710016 | bytes 48644448 | solution.py:77
  575.2 1.9 fusion.68
  577.8 1.4 fusion.69
  586.8 1.9 fusion.68
  598.4 1.9 fusion.68
  610.1 1.9 fusion.68
  612.7 1.4 fusion.69
  621.7 1.9 fusion.68
  633.3 1.9 fusion.68
  635.9 1.4 fusion.69
  644.9 1.9 fusion.68
  656.5 1.9 fusion.68
  665.3 1.6 copy.40
  668.3 1.4 maximum_select_fusion
  669.8 2.5 broadcast_in_dim.68
  672.2 6.4 scatter_fusion
  678.6 7.4 all-to-all-start
  686.1 186.6 %all-reduce = f32[512]{0:T(512)S(1)} all-reduce(f32[512]{0:T(512)S(1)} %dynamic-update-slice), channel_id=1, replica_groups=mesh['ctx'=64,'tp'=8] {'ctx','tp'}, use_global_device_ids=true, to_apply=%add | all-reduce | flops 512 | bytes 4096
  875.3 2.4 reduce_sum.45
  (208 shorter events, 78.4 us)
Async XLA Ops:
  7.2 6.5 copy-start
  7.2 9.2 %copy-start.8 = (bf16[256,1024]{1,0:T(8,128)(2,1)S(1)}, bf16[256,1024]{1,0:T(8,128)(2,1)}, u32[]{:S(2)}) copy-start(bf16[256,1024]{1,0:T(8,128)(2,1)} %param.12) | copy-start | bytes 1572868
  7.2 263.5 %all-gather.5.cloned.1.call-start = ((), (), s32[]{:S(2)}) async-start(), calls=%async_computation.2 | async-start | bytes 1064960 | tf_op jit(solution)/shard_map/all_gather | solution.py:21
  7.9 562.4 %all-gather.3.cloned.1.call-start = ((), (), s32[]{:S(2)}) async-start(), calls=%async_computation.1 | async-start | bytes 1064960 | tf_op jit(solution)/shard_map/all_gather | solution.py:20
  579.3 2.5 copy-start.4
  580.7 2.4 copy-start.2
  580.7 3.4 copy-start.7
  590.9 2.5 copy-start.4
  592.3 3.4 copy-start.7
  602.5 2.5 copy-start.4
  603.9 2.4 copy-start.2
  603.9 3.4 copy-start.7
  614.1 2.5 copy-start.4
  615.5 3.4 copy-start.7
  625.7 2.5 copy-start.4
  627.1 3.4 copy-start.7
  637.3 2.5 copy-start.4
  638.7 3.4 copy-start.7
  649.0 2.5 copy-start.4
  650.4 3.4 copy-start.7
  660.6 2.5 copy-start.4
  662.0 3.4 copy-start.7
  678.6 194.7 %copy-start.9 = (bf16[8,256,1,128]{3,1,2,0:T(8,128)(2,1)S(1)}, bf16[8,256,1,128]{3,1,2,0:T(8,128)(2,1)}, u32[]{:S(2)}) copy-start(bf16[8,256,1,128]{3,1,2,0:T(8,128)(2,1)} %get-tuple-element.69) | copy-start | bytes 1572868
  678.6 196.6 %all-to-all-start = ((f32[64,64,256]{2,1,0:T(8,128)}), f32[64,64,256]{2,1,0:T(8,128)}, u32[]{:S(2)}, u32[]{:S(2)}) async-start(f32[64,64,256]{2,1,0:T(8,128)} %scatter_fusion), calls=%async_computation | async-start | bytes 8388608 | tf_op jit(solution)/shard_map/all_to_all | solution.py:92
  (31 other events, 46.7 us)
Sparse Core Ops, SparseCore 0:
  10.1 260.5 all-gather.4
  272.8 297.4 all-gather.2
